TPU v7x, 512 devices: a whole 4x4x16 slice. The times are simulated.
512 devices in a mesh: dp: 64 (over x, z), mp: 8 (over y, core).
Axes of the slice: x: 4, y: 4, z: 16, core: 2. Of those that a mesh axis runs over, the one named last changes fastest.
Arguments:
- activations: bfloat16 [16384, 512], P('dp'), may hold values from -6 to 6
- cotangent: bfloat16 [16384, 24576], P('dp', 'mp'), may hold values from -0.375 to 0.375
- block_scale: bfloat16 [32768, 192], P('dp', 'mp'), may hold values from 0.0009994507 to 0.049804688
- master_weight: float32 [512, 24576], P('dp', 'mp'), may hold values from -6 to 6
- moment_one: float32 [512, 24576], P('dp', 'mp'), may hold values from -4 to 4
- moment_two: float32 [512, 24576], P('dp', 'mp'), may hold values from 0.05 to 2
Outputs:
- new_weight: bfloat16 [512, 24576], P('dp')
- master_out: float32 [512, 24576], P('dp', 'mp')
- moment_one_out: float32 [512, 24576], P('dp', 'mp')
- moment_two_out: float32 [512, 24576], P('dp', 'mp')
All inputs are finite; a program needn't handle non-finite values.
Results may differ from a plain program's by a relative error of at most 0.0026.
Values may be sent and summed in bfloat16 or wider, within the bound.
A program may use at most 64 MiB of HBM per device.

v0:
```python
import jax
import jax.numpy as jnp
from jax import lax
from jax.sharding import PartitionSpec as P

bias_one = 0.9999734386011124
bias_two = 0.994079470779666


def hadamard_table():
    indices = jnp.arange(128, dtype=jnp.int32)
    anded = jnp.bitwise_and(indices[:, None], indices[None, :])
    parity = jnp.zeros((128, 128), jnp.int32)
    for shift in range(7):
        parity = parity + jnp.bitwise_and(jnp.right_shift(anded, shift), 1)
    signs = 1 - 2 * jnp.bitwise_and(parity, 1)
    return signs.astype(jnp.float32) / jnp.sqrt(jnp.float32(128.0))


def rotate(matrix, table):
    lead_shape = matrix.shape[:-1]
    col_count = matrix.shape[-1]
    blocks = matrix.reshape(lead_shape + (col_count // 128, 128))
    turned = jnp.einsum("...bk,kj->...bj", blocks, table, precision=lax.Precision.HIGHEST)
    return turned.reshape(lead_shape + (col_count,))


def quantize(matrix, scales, table):
    row_count, col_count = matrix.shape
    blocks = rotate(matrix, table).reshape(row_count, col_count // 128, 128)
    scaled = blocks / scales.astype(jnp.float32)[:, :, None]
    quant = jnp.clip(scaled, -448.0, 448.0).astype(jnp.bfloat16)
    return quant.reshape(row_count, col_count)


def combine(received, got_scales, sources, table):
    row_total, col_count = received.shape
    own_rows = row_total // sources
    blocks = received.reshape(sources, own_rows, col_count // 128, 128).astype(jnp.float32)
    restored = blocks * got_scales.reshape(sources, own_rows, col_count // 128)[
        :, :, :, None
    ].astype(jnp.float32)
    restored = restored.reshape(sources, own_rows, col_count)
    return rotate(jnp.sum(restored, axis=0), table)


def local_gradient(activations, cot_part):
    return lax.dot_general(
        activations, cot_part, (((0,), (0,)), ((), ())), preferred_element_type=jnp.float32
    )


def local(activations, cotangent, block_scale, master_weight, moment_one, moment_two):
    table = hadamard_table()
    sources = lax.axis_size("dp")
    quant = quantize(local_gradient(activations, cotangent), block_scale, table)
    received, got_scales = (
        lax.all_to_all(quant, "dp", split_axis=0, concat_axis=0, tiled=True),
        lax.all_to_all(block_scale, "dp", split_axis=0, concat_axis=0, tiled=True),
    )
    gradient = combine(received, got_scales, sources, table)
    moment_one_out = 0.9 * moment_one + 0.1 * gradient
    moment_two_out = 0.95 * moment_two + 0.05 * gradient * gradient
    first_hat = moment_one_out / bias_one
    second_hat = moment_two_out / bias_two
    master_out = master_weight - 0.01 * (
        first_hat / (jnp.sqrt(second_hat) + 1e-08) + 0.1 * master_weight
    )
    new_weight = lax.all_gather(master_out.astype(jnp.bfloat16), "mp", axis=1, tiled=True)
    return (new_weight, master_out, moment_one_out, moment_two_out)


def solution(mesh):
    return jax.shard_map(
        local,
        mesh=mesh,
        in_specs=(
            P("dp", None),
            P("dp", "mp"),
            P("dp", "mp"),
            P("dp", "mp"),
            P("dp", "mp"),
            P("dp", "mp"),
        ),
        out_specs=(P("dp", None), P("dp", "mp"), P("dp", "mp"), P("dp", "mp")),
        check_vma=False,
    )
```

profile of v0, /device:TPU:1, one launch (start us, length us, event | category | flops | bytes accessed | tf_op | source)
XLA Modules:
  0.0 217.2 jit_solution(14675384311430281759)
XLA Ops:
  0.6 0.0 copy-start
  0.6 1.6 copy.23
  2.3 19.1 %all-to-all-start.1 = ((bf16[64,8,24]{2,1,0:T(8,128)(2,1)}), bf16[64,8,24]{2,1,0:T(8,128)(2,1)S(1)}, u32[]{:S(2)}, u32[]{:S(2)}) async-start(bf16[64,8,24]{2,1,0:T(8,128)(2,1)} %bitcast.1), calls=%async_computation.1 | async-start | bytes 262144 | tf_op jit(solution)/shard_map/all_to_all | solution.py:59
  21.4 0.7 convert_element_type.27
  22.1 0.0 copy-done
  22.1 2.0 convolution_bitcast_fusion
  24.1 5.4 %clamp_convert_fusion = bf16[512,24,128]{2,0,1:T(8,128)(2,1)S(1)} fusion(f32[512,24]{0,1:T(8,128)S(1)} %convert_element_type.27, f32[64,24,8,128]{3,2,1,0:T(8,128)S(1)} %convolution_bitcast_fusion), kind=kOutput, calls=%fused_computation.5 | convolution fusion | flops 2421063680 | bytes 9486336 | tf_op jit(solution)/shard_map/...bk,kj->...bj/dot_general | solution.py:24
  29.5 3.7 %copy.22 = bf16[512,24,128]{2,1,0:T(8,128)(2,1)} copy(bf16[512,24,128]{2,0,1:T(8,128)(2,1)S(1)} %clamp_convert_fusion) | data formatting | bytes 6291456 | tf_op jit(solution)/shard_map/convert_element_type | solution.py:32
  33.2 5.8 %all_to_all.12 = bf16[64,8,3072]{2,1,0:T(8,128)(2,1)} reshape(bf16[512,24,128]{2,1,0:T(8,128)(2,1)} %copy.22) | data formatting | bytes 6291456 | tf_op jit(solution)/shard_map/all_to_all | solution.py:58
  39.0 0.0 copy-start.1
  39.0 0.0 copy-start.2
  39.0 0.0 copy-start.3
  39.0 0.0 all-to-all-done.1
  39.0 14.9 %all-to-all-start = ((bf16[64,8,3072]{2,1,0:T(8,128)(2,1)}), bf16[64,8,3072]{2,1,0:T(8,128)(2,1)}, u32[]{:S(2)}, u32[]{:S(2)}) async-start(bf16[64,8,3072]{2,1,0:T(8,128)(2,1)} %all_to_all.12), calls=%async_computation | async-start | bytes 6291456 | tf_op jit(solution)/shard_map/all_to_all | solution.py:58
  54.0 0.1 copy.24
  54.1 0.3 copy.25
  54.4 136.9 %all-to-all-done = bf16[64,8,3072]{2,1,0:T(8,128)(2,1)} async-done(((bf16[64,8,3072]{2,1,0:T(8,128)(2,1)}), bf16[64,8,3072]{2,1,0:T(8,128)(2,1)}, u32[]{:S(2)}, u32[]{:S(2)}) %all-to-all-start) | async-done | bytes 3145760 | tf_op jit(solution)/shard_map/all_to_all | solution.py:58
  191.3 3.8 %fusion.3 = f32[8,3072]{1,0:T(8,128)S(1)} fusion(bf16[64,8,3072]{2,1,0:T(8,128)(2,1)} %all-to-all-done, f32[64,8,24]{1,2,0:T(8,128)S(1)} %copy.25), kind=kLoop, calls=%fused_computation.4 | loop fusion | flops 4694016 | bytes 3293184 | tf_op jit(solution)/shard_map/reduce_sum | solution.py:44
  195.1 0.3 convolution_bitcast_fusion.1
  195.4 0.0 copy-done.1
  195.4 0.0 copy-done.2
  195.4 0.0 copy-done.3
  195.4 0.8 fusion.28
  196.2 20.3 %all_gather.3 = bf16[8,24576]{1,0:T(8,128)(2,1)S(1)} all-gather(bf16[8,3072]{1,0:T(8,128)(2,1)S(1)} %get-tuple-element.4), channel_id=1, replica_groups=mesh['dp'=64,'mp'=8] {'mp'}, dimensions={1}, use_global_device_ids=true | all-gather | bytes 442368 | tf_op jit(solution)/shard_map/all_gather | solution.py:69
  216.4 0.7 copy.44
Async XLA Ops:
  0.6 21.5 %copy-start = (bf16[256,3072]{1,0:T(8,128)(2,1)S(1)}, bf16[256,3072]{1,0:T(8,128)(2,1)}, u32[]{:S(2)}) copy-start(bf16[256,3072]{1,0:T(8,128)(2,1)} %param.7) | copy-start | bytes 4718596
  2.3 36.8 %all-to-all-start.1 = ((bf16[64,8,24]{2,1,0:T(8,128)(2,1)}), bf16[64,8,24]{2,1,0:T(8,128)(2,1)S(1)}, u32[]{:S(2)}, u32[]{:S(2)}) async-start(bf16[64,8,24]{2,1,0:T(8,128)(2,1)} %bitcast.1), calls=%async_computation.1 | async-start | bytes 262144 | tf_op jit(solution)/shard_map/all_to_all | solution.py:59
  39.0 156.4 %copy-start.1 = (f32[8,3072]{1,0:T(8,128)S(1)}, f32[8,3072]{1,0:T(8,128)}, u32[]{:S(2)}) copy-start(f32[8,3072]{1,0:T(8,128)} %param.9) | copy-start | bytes 294916
  39.0 156.4 %copy-start.2 = (f32[8,3072]{1,0:T(8,128)S(1)}, f32[8,3072]{1,0:T(8,128)}, u32[]{:S(2)}) copy-start(f32[8,3072]{1,0:T(8,128)} %param.10) | copy-start | bytes 294916
  39.0 156.4 %copy-start.3 = (f32[8,3072]{1,0:T(8,128)S(1)}, f32[8,3072]{1,0:T(8,128)}, u32[]{:S(2)}) copy-start(f32[8,3072]{1,0:T(8,128)} %param.11) | copy-start | bytes 294916
  39.0 152.3 %all-to-all-start = ((bf16[64,8,3072]{2,1,0:T(8,128)(2,1)}), bf16[64,8,3072]{2,1,0:T(8,128)(2,1)}, u32[]{:S(2)}, u32[]{:S(2)}) async-start(bf16[64,8,3072]{2,1,0:T(8,128)(2,1)} %all_to_all.12), calls=%async_computation | async-start | bytes 6291456 | tf_op jit(solution)/shard_map/all_to_all | solution.py:58
where the time goes:
time: 218 us; the launch traced here: 217 us
  waiting for transfers between devices  137 us (63%)
  starting transfers between devices  34 us (16%)
  blocking collectives  20.3 us (9%)
  local copies, waits for them, and re-layouts  12.3 us (6%)
  matrix products  7.62 us (3%)
  other arithmetic  5.26 us (2%)
    all_to_all x1, waiting for transfers between devices, local(): lax.all_to_all(quant, 'dp', split_axis=0, concat_axis=0, tiled=True)  137 us
    all_gather x1, blocking collectives, local(): lax.all_gather(master_out.astype(jnp.bfloat16), 'mp', axis=1, tiled=True)  20.3 us
    all_to_all x1, starting transfers between devices, local(): lax.all_to_all(block_scale, 'dp', split_axis=0, concat_axis=0, tiled=True)  19.1 us
    all_to_all x1, starting transfers between devices, local(): lax.all_to_all(quant, 'dp', split_axis=0, concat_axis=0, tiled=True)  14.9 us
    all_to_all x1, local copies, waits for them, and re-layouts, local(): lax.all_to_all(quant, 'dp', split_axis=0, concat_axis=0, tiled=True)  5.83 us
    dot_general x2, matrix products, rotate(): jnp.einsum('...bk,kj->...bj', blocks, table, precision=lax.Precision.HIGH...  5.67 us
  transfers between devices with their start and end apart: 2, of which 1 were waited for; matrix products, arithmetic and copies ran while one was open for 6% of the time, Pallas kernels for 0%

commit v1 on v0

v1 whole, which is shorter than its diff:
```python
import functools
import math

import jax
import jax.numpy as jnp
from jax import lax
from jax.experimental import pallas as pl
from jax.experimental.pallas import tpu as pltpu
from jax.sharding import PartitionSpec as P

BIAS_ONE = 0.9999734386011124
BIAS_TWO = 0.994079470779666
NX, NZ, NMP = 4, 16, 8
ROWS = 8
COLS = 3072
BLOCKS = COLS // 128
CHUNKS = 4
W = COLS // CHUNKS
TILE = 256
HALF = NZ // 2
UNIT = 2.0**20
ROOT = 1.0 / math.sqrt(128.0)
F32, BF16 = jnp.float32, jnp.bfloat16


def encode(x):
    return ((x * jnp.abs(x)) * (x * x)).astype(BF16)


def decode(y):
    y = y.astype(F32)
    size = jnp.maximum(jnp.abs(y), 2.0**-124)
    r = lax.rsqrt(size)
    return y * (r * lax.rsqrt(size * r))


def split(x, parts):
    out = []
    for _ in range(parts):
        piece = x.astype(BF16)
        out.append(piece)
        x = x - piece.astype(F32)
    return out


def signs(size):
    i = lax.broadcasted_iota(jnp.int32, (size, size), 0)
    j = lax.broadcasted_iota(jnp.int32, (size, size), 1)
    both = i & j
    odd = both & 1
    for bit in range(1, 7):
        odd = odd ^ ((both >> bit) & 1)
    same = (i >> 7) == (j >> 7)
    return jnp.where(same, (1 - 2 * odd).astype(F32), 0.0).astype(BF16)


def dot(a, b):
    return lax.dot_general(a, b, (((1,), (0,)), ((), ())), preferred_element_type=F32)


def kernel(
    act_ref, cot_ref, scale_ref, master_ref, one_ref, two_ref,
    weight_out, master_out, one_out, two_out,
    act_t, scale_t, table, values, ring_out, ring_in, x_out, x_in, w_out, w_in,
    ring_ss, ring_rs, x_ss, x_rs, w_ss, w_rs,
):
    dp, mp = lax.axis_index("dp"), lax.axis_index("mp")
    x, z = dp // NZ, lax.rem(dp, NZ)

    def at_z(step):
        return {"dp": x * NZ + lax.rem(z + step + NZ, NZ)}

    def at_x(step):
        return {"dp": lax.rem(x + step + NX, NX) * NZ + z}

    def at_mp(step):
        return {"mp": lax.rem(mp + step + NMP, NMP)}

    barrier = pltpu.get_barrier_semaphore()
    partners = [at_z(1), at_z(-1)]
    partners += [at_x(j) for j in range(1, NX)] + [at_mp(j) for j in range(1, NMP)]
    for partner in partners:
        pl.semaphore_signal(barrier, inc=1, device_id=partner)

    act_t[...] = act_ref[...].astype(F32).T.astype(BF16)
    scale = scale_ref[...].astype(F32)
    parts = [p.astype(F32) for p in split(ROOT / scale, 3)]
    pad = jnp.zeros((128 - 4 * BLOCKS, NX * NZ * ROWS), F32)
    scale_t[...] = jnp.concatenate([scale] + parts + [pad], axis=0).T.astype(BF16)
    table[...] = signs(TILE)

    def local_tile(tile):
        cols = pl.ds(pl.multiple_of(tile * TILE, TILE), TILE)
        turned = split(dot(cot_ref[:, cols], table[...]), 2)
        k = lax.broadcasted_iota(jnp.int32, (128, 2 * TILE), 0)
        n = lax.broadcasted_iota(jnp.int32, (128, 2 * TILE), 1)
        block = tile * (TILE // 128) + ((n >> 7) & (TILE // 128 - 1))
        in_scale = jnp.where(k == block, UNIT, 0.0)
        hit = (k == block + BLOCKS) | (k == block + 2 * BLOCKS) | (k == block + 3 * BLOCKS)
        pick = jnp.where(n < TILE, in_scale, jnp.where(hit, 1.0, 0.0)).astype(BF16)
        for part in range(NX):
            rows = slice(part * NZ * ROWS, (part + 1) * NZ * ROWS)
            a = act_t[rows, :]
            grad = dot(a, turned[0]) + dot(a, turned[1])
            both = dot(scale_t[rows, :], pick)
            quant = jnp.clip(grad * both[:, TILE:], -448.0, 448.0).astype(BF16)
            values[part, :, :, cols] = (quant.astype(F32) * both[:, :TILE]).reshape(NZ, ROWS, TILE)

    def ring_copy(c, d, s, width=W):
        return pltpu.make_async_remote_copy(
            src_ref=ring_out.at[c, d, s, :, pl.ds(0, width)],
            dst_ref=ring_in.at[c, d, s, :, pl.ds(0, width)],
            send_sem=ring_ss.at[c, d, s],
            recv_sem=ring_rs.at[c, d, s],
            device_id=at_z(1 - 2 * d),
        )

    def own(c, zd, lo):
        return values[:, zd, :, c * W + lo : c * W + lo + 128].reshape(NX * ROWS, 128)

    def target(d, s):
        return lax.rem(z + (1 - 2 * d) * (HALF - s) + NZ, NZ)

    def first(c):
        for d in range(2):
            zd = target(d, 0)
            for lo in range(0, W // 2, 128):
                ring_out[c, d, 0, :, lo : lo + 128] = encode(own(c, zd, lo + d * (W // 2)))
            ring_copy(c, d, 0, W // 2).start()

    def pass_on(c, d, s, half):
        zd = target(d, s)
        ring_copy(c, d, s - 1, W // 2 if half else W).wait_recv()
        for lo in range(0, W, 128):
            total = own(c, zd, lo)
            if not half:
                total = total + decode(ring_in[c, d, s - 1, :, lo : lo + 128])
            elif lo // (W // 2) == d:
                at = lo - d * (W // 2)
                total = total + decode(ring_in[c, d, 0, :, at : at + 128])
            ring_out[c, d, s, :, lo : lo + 128] = encode(total)
        ring_copy(c, d, s).start()

    def x_copy(c, j):
        return pltpu.make_async_remote_copy(
            src_ref=x_out.at[c, lax.rem(x + j, NX)],
            dst_ref=x_in.at[c, j - 1],
            send_sem=x_ss.at[c, j - 1],
            recv_sem=x_rs.at[c, j - 1],
            device_id=at_x(j),
        )

    def w_copy(c, j, slot):
        return pltpu.make_async_remote_copy(
            src_ref=w_out.at[c],
            dst_ref=w_in.at[c, slot],
            send_sem=w_ss.at[c, j - 1],
            recv_sem=w_rs.at[c, slot],
            device_id=at_mp(j),
        )

    per = W // TILE
    for c in range(CHUNKS):
        lax.fori_loop(c * per, (c + 1) * per, lambda t, _: (local_tile(t), 0)[1], 0)
        if c == 0:
            pl.semaphore_wait(barrier, len(partners))
        first(c)
    for c in range(CHUNKS):
        for d in range(2):
            pass_on(c, d, 1, True)

    def step(s, carry):
        for c in range(CHUNKS):
            for d in range(2):
                pass_on(c, d, s, False)
        return carry

    lax.fori_loop(2, HALF, step, 0)

    for c in range(CHUNKS):
        for d in range(2):
            ring_copy(c, d, HALF - 1).wait_recv()
        for lo in range(0, W, 128):
            total = own(c, z, lo) + decode(ring_in[c, 0, HALF - 1, :, lo : lo + 128])
            total = total + decode(ring_in[c, 1, HALF - 1, :, lo : lo + 128])
            x_out[c, :, :, lo : lo + 128] = total.reshape(NX, ROWS, 128)
        for j in range(1, NX):
            x_copy(c, j).start()

    for c in range(CHUNKS):
        for j in range(1, NX):
            x_copy(c, j).wait_recv()
        total = x_out[c, x]
        for j in range(1, NX):
            total = total + x_in[c, j - 1]
        stack = jnp.concatenate([total[:, lo : lo + 128] for lo in range(0, W, 128)], axis=0)
        pieces = split(stack, 3)
        turned = dot(pieces[0], table[:128, :128])
        turned = turned + dot(pieces[1], table[:128, :128])
        turned = (turned + dot(pieces[2], table[:128, :128])) * (ROOT / UNIT)
        blocks = []
        for b in range(W // 128):
            cols = slice(c * W + b * 128, c * W + (b + 1) * 128)
            gradient = turned[b * ROWS : (b + 1) * ROWS, :]
            one = 0.9 * one_ref[:, cols] + 0.1 * gradient
            two = 0.95 * two_ref[:, cols] + 0.05 * gradient * gradient
            master = master_ref[:, cols]
            change = (one / BIAS_ONE) / (jnp.sqrt(two / BIAS_TWO) + 1e-08)
            master = master - 0.01 * (change + 0.1 * master)
            one_out[:, cols] = one
            two_out[:, cols] = two
            master_out[:, cols] = master
            blocks.append(master)
        for b in range(W // 256):
            pair = jnp.concatenate([blocks[b], blocks[b + W // 256]], axis=0).astype(BF16)
            w_out[c, :, b * 128 : (b + 1) * 128] = pair
        for j in range(1, NMP):
            w_copy(c, j, mp).start()

    for c in range(CHUNKS):
        w_in[c, mp] = w_out[c]
        for j in range(1, NMP):
            w_copy(c, j, lax.rem(mp - j + NMP, NMP)).wait_recv()
        for source in range(NMP):
            both = w_in[c, source].astype(F32)
            at = source * COLS + c * W
            weight_out[:, at : at + W // 2] = both[:ROWS].astype(BF16)
            weight_out[:, at + W // 2 : at + W] = both[ROWS:].astype(BF16)

    for c in range(CHUNKS):
        for d in range(2):
            ring_copy(c, d, 0, W // 2).wait_send()
            lax.fori_loop(1, HALF, lambda s, _: (ring_copy(c, d, s).wait_send(), 0)[1], 0)
        for j in range(1, NX):
            x_copy(c, j).wait_send()
        for j in range(1, NMP):
            w_copy(c, j, mp).wait_send()


def local(activations, cotangent, block_scale, master_weight, moment_one, moment_two):
    vmem = pl.BlockSpec(memory_space=pltpu.VMEM)
    rows = NX * NZ * ROWS
    state = jax.ShapeDtypeStruct((ROWS, COLS), F32)
    dma = pltpu.SemaphoreType.DMA
    return pl.pallas_call(
        kernel,
        out_shape=(jax.ShapeDtypeStruct((ROWS, COLS * NMP), BF16), state, state, state),
        in_specs=[vmem] * 6,
        out_specs=(vmem,) * 4,
        scratch_shapes=[
            pltpu.VMEM((rows, 256), BF16),
            pltpu.VMEM((rows, 128), BF16),
            pltpu.VMEM((TILE, TILE), BF16),
            pltpu.VMEM((NX, NZ, ROWS, COLS), F32),
            pltpu.VMEM((CHUNKS, 2, HALF, NX * ROWS, W), BF16),
            pltpu.VMEM((CHUNKS, 2, HALF, NX * ROWS, W), BF16),
            pltpu.VMEM((CHUNKS, NX, ROWS, W), F32),
            pltpu.VMEM((CHUNKS, NX - 1, ROWS, W), F32),
            pltpu.VMEM((CHUNKS, 2 * ROWS, W // 2), BF16),
            pltpu.VMEM((CHUNKS, NMP, 2 * ROWS, W // 2), BF16),
            dma((CHUNKS, 2, HALF)),
            dma((CHUNKS, 2, HALF)),
            dma((CHUNKS, NX - 1)),
            dma((CHUNKS, NX - 1)),
            dma((CHUNKS, NMP - 1)),
            dma((CHUNKS, NMP)),
        ],
        compiler_params=pltpu.CompilerParams(
            collective_id=0, has_side_effects=True, vmem_limit_bytes=48 * 2**20
        ),
        cost_estimate=pl.CostEstimate(flops=3 * 10**9, bytes_accessed=4 * 10**6, transcendentals=0),
    )(activations, cotangent, block_scale.T, master_weight, moment_one, moment_two)


def solution(mesh):
    return jax.shard_map(
        local,
        mesh=mesh,
        in_specs=(P("dp", None),) + (P("dp", "mp"),) * 5,
        out_specs=(P("dp", None),) + (P("dp", "mp"),) * 3,
        check_vma=False,
    )
```

time: 218 us -> 73.3 us (0.34)
  waiting for transfers between devices: 137 us -> 0 us
  Pallas kernels: 0 us -> 63.9 us
  starting transfers between devices: 34 us -> 0 us
  blocking collectives: 20.3 us -> 0 us
  matrix products: 7.62 us -> 0 us
  other arithmetic: 5.26 us -> 0 us
  local copies, waits for them, and re-layouts: 12.3 us -> 8.43 us
    all_to_all x2 -> x0, waiting for transfers between devices: 137 us -> none  [the longest x1 137 us: local(): lax.all_to_all(quant, 'dp', split_axis=0, concat_axis=0, tiled=True)]
    pallas_call x0 -> x1, Pallas kernels: none -> 63.9 us  [local(): pl.pallas_call(kernel, out_shape=(jax.ShapeDtypeStruct((ROWS, COLS * NMP)...]
    all_to_all x2 -> x0, starting transfers between devices: 34 us -> none  [the longest x1 19.1 us: local(): lax.all_to_all(block_scale, 'dp', split_axis=0, concat_axis=0, tiled=True)]
    all_gather x1 -> x0, blocking collectives: 20.3 us -> none  [local(): lax.all_gather(master_out.astype(jnp.bfloat16), 'mp', axis=1, tiled=True)]
    dot_general x3 -> x0, matrix products: 7.62 us -> none  [the longest x2 5.67 us: rotate(): jnp.einsum('...bk,kj->...bj', blocks, table, precision=lax.Precision.HIGH...]
    unnamed x10 -> x16, local copies, waits for them, and re-layouts: 2.38 us -> 8.43 us
    all_to_all x2 -> x0, local copies, waits for them, and re-layouts: 5.96 us -> none  [the longest x1 5.83 us: local(): lax.all_to_all(quant, 'dp', split_axis=0, concat_axis=0, tiled=True)]
    convert_element_type x2 -> x0, local copies, waits for them, and re-layouts: 3.98 us -> none  [the longest x1 3.71 us: quantize(): quant = jnp.clip(scaled, -448.0, 448.0).astype(jnp.bfloat16)]
  transfers between devices with their start and end apart: 2 -> 0, of which waited for: 1 -> 0; matrix products, arithmetic and copies ran while one was open for 6% -> 0% of each run, Pallas kernels for 0% -> 0%
where the time goes in v1:
time: 73.3 us; the launch traced here: 73 us
  Pallas kernels  63.9 us (87%)
  local copies, waits for them, and re-layouts  8.43 us (12%)
    pallas_call x1, Pallas kernels, local(): pl.pallas_call(kernel, out_shape=(jax.ShapeDtypeStruct((ROWS, COLS * NMP)...  63.9 us
    unnamed x16, local copies, waits for them, and re-layouts  8.43 us

profile of v1, /device:TPU:1, one launch (start us, length us, event | category | flops | bytes accessed | tf_op | source)
XLA Modules:
  0.0 73.0 jit_solution(18229524362788445202)
XLA Ops:
  0.6 0.0 copy-start
  0.6 1.4 %copy-done = bf16[256,3072]{1,0:T(8,128)(2,1)S(1)} copy-done((bf16[256,3072]{1,0:T(8,128)(2,1)S(1)}, bf16[256,3072]{1,0:T(8,128)(2,1)}, u32[]{:S(2)}) %copy-start) | copy-done | bytes 1572888
  2.0 0.0 copy-start.1
  2.0 0.9 %copy-done.1 = bf16[256,512]{1,0:T(8,128)(2,1)S(1)} copy-done((bf16[256,512]{1,0:T(8,128)(2,1)S(1)}, bf16[256,512]{1,0:T(8,128)(2,1)}, u32[]{:S(2)}) %copy-start.1) | copy-done | bytes 262168
  3.0 0.0 copy-start.2
  3.0 0.9 %copy-done.2 = f32[8,3072]{1,0:T(8,128)S(1)} copy-done((f32[8,3072]{1,0:T(8,128)S(1)}, f32[8,3072]{1,0:T(8,128)}, u32[]{:S(2)}) %copy-start.2) | copy-done | bytes 98328
  3.9 0.0 copy-start.3
  3.9 0.9 %copy-done.3 = f32[8,3072]{1,0:T(8,128)S(1)} copy-done((f32[8,3072]{1,0:T(8,128)S(1)}, f32[8,3072]{1,0:T(8,128)}, u32[]{:S(2)}) %copy-start.3) | copy-done | bytes 98328
  4.8 0.0 copy-start.4
  4.8 0.9 %copy-done.4 = f32[8,3072]{1,0:T(8,128)S(1)} copy-done((f32[8,3072]{1,0:T(8,128)S(1)}, f32[8,3072]{1,0:T(8,128)}, u32[]{:S(2)}) %copy-start.4) | copy-done | bytes 98328
  5.7 0.0 copy-start.5
  5.7 0.7 %copy-done.5 = bf16[512,24]{0,1:T(8,128)(2,1)S(1)} copy-done((bf16[512,24]{0,1:T(8,128)(2,1)S(1)}, bf16[512,24]{0,1:T(8,128)(2,1)}, u32[]{:S(2)}) %copy-start.5) | copy-done | bytes 24600
  6.4 63.9 %shard_map.93 = (bf16[8,24576]{1,0:T(8,128)(2,1)S(1)}, f32[8,3072]{1,0:T(8,128)S(1)}, f32[8,3072]{1,0:T(8,128)S(1)}, f32[8,3072]{1,0:T(8,128)S(1)}) custom-call(bf16[256,512]{1,0:T(8,128)(2,1)S(1)} %copy-done.1, bf16[256,3072]{1,0:T(8,128)(2,1)S(1)} %copy-done, bf16[24,512]{1,0:T(8,128)(2,1)S(1)} %bitcast.1, f32[8,3072]{1,0:T(8,128)S(1)} %copy-done.2, ...), custom_call_target="tpu_custom_call" | custom-call | flops 3000000000 | bytes 4000000 | tf_op jit(solution)/shard_map/pallas_call | solution.py:245
  70.3 0.7 %copy.14 = bf16[8,24576]{1,0:T(8,128)(2,1)} copy(bf16[8,24576]{1,0:T(8,128)(2,1)S(1)} %get-tuple-element.8) | data formatting | bytes 786432
  71.1 0.6 copy.15
  71.7 0.6 copy.16
  72.3 0.6 copy.17
Async XLA Ops:
  0.6 1.4 %copy-start = (bf16[256,3072]{1,0:T(8,128)(2,1)S(1)}, bf16[256,3072]{1,0:T(8,128)(2,1)}, u32[]{:S(2)}) copy-start(bf16[256,3072]{1,0:T(8,128)(2,1)} %cot_ref.1) | copy-start | bytes 4718596
  2.0 0.9 %copy-start.1 = (bf16[256,512]{1,0:T(8,128)(2,1)S(1)}, bf16[256,512]{1,0:T(8,128)(2,1)}, u32[]{:S(2)}) copy-start(bf16[256,512]{1,0:T(8,128)(2,1)} %act_ref.1) | copy-start | bytes 786436
  3.0 0.9 %copy-start.2 = (f32[8,3072]{1,0:T(8,128)S(1)}, f32[8,3072]{1,0:T(8,128)}, u32[]{:S(2)}) copy-start(f32[8,3072]{1,0:T(8,128)} %master_ref.1) | copy-start | bytes 294916
  3.9 0.9 %copy-start.3 = (f32[8,3072]{1,0:T(8,128)S(1)}, f32[8,3072]{1,0:T(8,128)}, u32[]{:S(2)}) copy-start(f32[8,3072]{1,0:T(8,128)} %one_ref.1) | copy-start | bytes 294916
  4.8 0.9 %copy-start.4 = (f32[8,3072]{1,0:T(8,128)S(1)}, f32[8,3072]{1,0:T(8,128)}, u32[]{:S(2)}) copy-start(f32[8,3072]{1,0:T(8,128)} %two_ref.1) | copy-start | bytes 294916
  5.7 0.7 %copy-start.5 = (bf16[512,24]{0,1:T(8,128)(2,1)S(1)}, bf16[512,24]{0,1:T(8,128)(2,1)}, u32[]{:S(2)}) copy-start(bf16[512,24]{0,1:T(8,128)(2,1)} %param.8) | copy-start | bytes 73732

commit v2 on v1

--- a/solution.py
+++ b/solution.py
@@ -12,6 +12,7 @@
 BIAS_TWO = 0.994079470779666
 NX, NZ, NMP = 4, 16, 8
 ROWS = 8
+GROUP = NX * ROWS
 COLS = 3072
 BLOCKS = COLS // 128
 CHUNKS = 4
@@ -59,10 +60,11 @@
 
 
 def kernel(
+    act_hbm, cot_hbm, scale_hbm, master_hbm, one_hbm, two_hbm,
+    weight_out, master_out, one_out, two_out,
     act_ref, cot_ref, scale_ref, master_ref, one_ref, two_ref,
-    weight_out, master_out, one_out, two_out,
-    act_t, scale_t, table, values, ring_out, ring_in, x_out, x_in, w_out, w_in,
-    ring_ss, ring_rs, x_ss, x_rs, w_ss, w_rs,
+    act_t, scale_t, table, turned, values, ring_out, ring_in, x_out, x_in, w_out, w_in,
+    load_sem, ring_ss, ring_rs, x_ss, x_rs, w_ss, w_rs,
 ):
     dp, mp = lax.axis_index("dp"), lax.axis_index("mp")
     x, z = dp // NZ, lax.rem(dp, NZ)
@@ -82,29 +84,51 @@
     for partner in partners:
         pl.semaphore_signal(barrier, inc=1, device_id=partner)
 
-    act_t[...] = act_ref[...].astype(F32).T.astype(BF16)
+    loads = [(act_hbm, act_ref), (scale_hbm, scale_ref)]
+    for c in range(CHUNKS):
+        cols = slice(c * W, (c + 1) * W)
+        loads.append((cot_hbm.at[:, cols], cot_ref.at[:, cols]))
+    loads += [(one_hbm, one_ref), (two_hbm, two_ref), (master_hbm, master_ref)]
+    loads = [pltpu.make_async_copy(s, d, load_sem.at[i]) for i, (s, d) in enumerate(loads)]
+    for load in loads:
+        load.start()
+
+    table[...] = signs(TILE)
+    loads[0].wait()
+    act = act_ref[...].astype(F32).T
+    for zd in range(NZ):
+        rows = [act[(xd * NZ + zd) * ROWS : (xd * NZ + zd + 1) * ROWS] for xd in range(NX)]
+        rows = jnp.concatenate(rows, axis=0).astype(BF16)
+        act_t[zd * GROUP : (zd + 1) * GROUP, :] = jnp.concatenate([rows, rows], axis=1)
+    loads[1].wait()
     scale = scale_ref[...].astype(F32)
-    parts = [p.astype(F32) for p in split(ROOT / scale, 3)]
-    pad = jnp.zeros((128 - 4 * BLOCKS, NX * NZ * ROWS), F32)
-    scale_t[...] = jnp.concatenate([scale] + parts + [pad], axis=0).T.astype(BF16)
-    table[...] = signs(TILE)
-
-    def local_tile(tile):
-        cols = pl.ds(pl.multiple_of(tile * TILE, TILE), TILE)
-        turned = split(dot(cot_ref[:, cols], table[...]), 2)
-        k = lax.broadcasted_iota(jnp.int32, (128, 2 * TILE), 0)
-        n = lax.broadcasted_iota(jnp.int32, (128, 2 * TILE), 1)
-        block = tile * (TILE // 128) + ((n >> 7) & (TILE // 128 - 1))
-        in_scale = jnp.where(k == block, UNIT, 0.0)
-        hit = (k == block + BLOCKS) | (k == block + 2 * BLOCKS) | (k == block + 3 * BLOCKS)
-        pick = jnp.where(n < TILE, in_scale, jnp.where(hit, 1.0, 0.0)).astype(BF16)
-        for part in range(NX):
-            rows = slice(part * NZ * ROWS, (part + 1) * NZ * ROWS)
-            a = act_t[rows, :]
-            grad = dot(a, turned[0]) + dot(a, turned[1])
-            both = dot(scale_t[rows, :], pick)
-            quant = jnp.clip(grad * both[:, TILE:], -448.0, 448.0).astype(BF16)
-            values[part, :, :, cols] = (quant.astype(F32) * both[:, :TILE]).reshape(NZ, ROWS, TILE)
+    pad = jnp.ones((128 - BLOCKS, NX * NZ * ROWS), F32)
+    scale = jnp.concatenate([scale, pad], axis=0).T
+    for zd in range(NZ):
+        for xd in range(NX):
+            at = (xd * NZ + zd) * ROWS
+            scale_t[zd * GROUP + xd * ROWS : zd * GROUP + (xd + 1) * ROWS, :] = scale[at : at + ROWS]
+    for c in range(CHUNKS):
+        loads[2 + c].wait()
+        for lo in range(c * W, (c + 1) * W, TILE):
+            high, low = split(dot(cot_ref[:, lo : lo + TILE], table[...]), 2)
+            turned[:256, lo : lo + TILE] = high
+            turned[256:, lo : lo + TILE] = low
+
+    def local_rows(targets):
+        spans = [pl.ds(pl.multiple_of(zd * GROUP, GROUP), GROUP) for zd in targets]
+        rows = jnp.concatenate([act_t[span, :] for span in spans], axis=0)
+        scales = jnp.concatenate([scale_t[span, :] for span in spans], axis=0)
+        inverse = ROOT / scales
+        for lo in range(0, COLS, TILE):
+            grad = dot(rows, turned[:, lo : lo + TILE])
+            for at in range(0, TILE, 128):
+                b = (lo + at) // 128
+                scaled = grad[:, at : at + 128] * inverse[:, b : b + 1]
+                quant = jnp.clip(scaled, -448.0, 448.0).astype(BF16).astype(F32)
+                value = quant * (scales[:, b : b + 1] * UNIT)
+                for i, zd in enumerate(targets):
+                    values[zd, :, lo + at : lo + at + 128] = value[i * GROUP : (i + 1) * GROUP]
 
     def ring_copy(c, d, s, width=W):
         return pltpu.make_async_remote_copy(
@@ -116,28 +140,27 @@
         )
 
     def own(c, zd, lo):
-        return values[:, zd, :, c * W + lo : c * W + lo + 128].reshape(NX * ROWS, 128)
+        return values[zd, :, c * W + lo : c * W + lo + 128]
 
     def target(d, s):
         return lax.rem(z + (1 - 2 * d) * (HALF - s) + NZ, NZ)
 
     def first(c):
+        zd = target(0, 0)
         for d in range(2):
-            zd = target(d, 0)
             for lo in range(0, W // 2, 128):
                 ring_out[c, d, 0, :, lo : lo + 128] = encode(own(c, zd, lo + d * (W // 2)))
             ring_copy(c, d, 0, W // 2).start()
 
-    def pass_on(c, d, s, half):
+    def pass_on(c, d, s, near=False):
         zd = target(d, s)
-        ring_copy(c, d, s - 1, W // 2 if half else W).wait_recv()
+        begin, width = (d * (W // 2), W // 2) if near else (0, W)
+        ring_copy(c, d, s - 1, width).wait_recv()
         for lo in range(0, W, 128):
             total = own(c, zd, lo)
-            if not half:
-                total = total + decode(ring_in[c, d, s - 1, :, lo : lo + 128])
-            elif lo // (W // 2) == d:
-                at = lo - d * (W // 2)
-                total = total + decode(ring_in[c, d, 0, :, at : at + 128])
+            if begin <= lo < begin + width:
+                at = lo - begin
+                total = total + decode(ring_in[c, d, s - 1, :, at : at + 128])
             ring_out[c, d, s, :, lo : lo + 128] = encode(total)
         ring_copy(c, d, s).start()
 
@@ -159,23 +182,22 @@
             device_id=at_mp(j),
         )
 
-    per = W // TILE
-    for c in range(CHUNKS):
-        lax.fori_loop(c * per, (c + 1) * per, lambda t, _: (local_tile(t), 0)[1], 0)
-        if c == 0:
-            pl.semaphore_wait(barrier, len(partners))
+    local_rows([target(0, 0)])
+    pl.semaphore_wait(barrier, len(partners))
+    for c in range(CHUNKS):
         first(c)
-    for c in range(CHUNKS):
-        for d in range(2):
-            pass_on(c, d, 1, True)
-
-    def step(s, carry):
+    local_rows([target(0, 1), target(1, 1)])
+    for load in loads[-3:]:
+        load.wait()
+
+    def step(s, near=False):
         for c in range(CHUNKS):
             for d in range(2):
-                pass_on(c, d, s, False)
-        return carry
-
-    lax.fori_loop(2, HALF, step, 0)
+                pass_on(c, d, s, near)
+        local_rows([target(0, s + 1), target(1, s + 1)])
+
+    step(1, True)
+    lax.fori_loop(2, HALF, lambda s, _: (step(s), 0)[1], 0)
 
     for c in range(CHUNKS):
         for d in range(2):
@@ -184,7 +206,7 @@
             total = own(c, z, lo) + decode(ring_in[c, 0, HALF - 1, :, lo : lo + 128])
             total = total + decode(ring_in[c, 1, HALF - 1, :, lo : lo + 128])
             x_out[c, :, :, lo : lo + 128] = total.reshape(NX, ROWS, 128)
-        for j in range(1, NX):
+        for j in (2, 1, 3):
             x_copy(c, j).start()
 
     for c in range(CHUNKS):
@@ -195,13 +217,13 @@
             total = total + x_in[c, j - 1]
         stack = jnp.concatenate([total[:, lo : lo + 128] for lo in range(0, W, 128)], axis=0)
         pieces = split(stack, 3)
-        turned = dot(pieces[0], table[:128, :128])
-        turned = turned + dot(pieces[1], table[:128, :128])
-        turned = (turned + dot(pieces[2], table[:128, :128])) * (ROOT / UNIT)
+        back = dot(pieces[0], table[:128, :128])
+        back = back + dot(pieces[1], table[:128, :128])
+        back = (back + dot(pieces[2], table[:128, :128])) * (ROOT / UNIT)
         blocks = []
         for b in range(W // 128):
             cols = slice(c * W + b * 128, c * W + (b + 1) * 128)
-            gradient = turned[b * ROWS : (b + 1) * ROWS, :]
+            gradient = back[b * ROWS : (b + 1) * ROWS, :]
             one = 0.9 * one_ref[:, cols] + 0.1 * gradient
             two = 0.95 * two_ref[:, cols] + 0.05 * gradient * gradient
             master = master_ref[:, cols]
@@ -216,9 +238,9 @@
             w_out[c, :, b * 128 : (b + 1) * 128] = pair
         for j in range(1, NMP):
             w_copy(c, j, mp).start()
-
-    for c in range(CHUNKS):
         w_in[c, mp] = w_out[c]
+
+    for c in range(CHUNKS):
         for j in range(1, NMP):
             w_copy(c, j, lax.rem(mp - j + NMP, NMP)).wait_recv()
         for source in range(NMP):
@@ -237,27 +259,46 @@
             w_copy(c, j, mp).wait_send()
 
 
+def write(*refs):
+    sources, outs, sem = refs[:4], refs[4:8], refs[8]
+    copies = [pltpu.make_async_copy(s, o, sem.at[i]) for i, (s, o) in enumerate(zip(sources, outs))]
+    for copy in copies:
+        copy.start()
+    for copy in copies:
+        copy.wait()
+
+
 def local(activations, cotangent, block_scale, master_weight, moment_one, moment_two):
-    vmem = pl.BlockSpec(memory_space=pltpu.VMEM)
+    vmem, hbm = pl.BlockSpec(memory_space=pltpu.VMEM), pl.BlockSpec(memory_space=pltpu.HBM)
     rows = NX * NZ * ROWS
-    state = jax.ShapeDtypeStruct((ROWS, COLS), F32)
     dma = pltpu.SemaphoreType.DMA
-    return pl.pallas_call(
+    args = (activations, cotangent, block_scale.T, master_weight, moment_one, moment_two)
+    args = [pltpu.with_memory_space_constraint(arg, pltpu.HBM) for arg in args]
+    shapes = (((ROWS, COLS * NMP), BF16),) + (((ROWS, COLS), F32),) * 3
+    results = pl.pallas_call(
         kernel,
-        out_shape=(jax.ShapeDtypeStruct((ROWS, COLS * NMP), BF16), state, state, state),
-        in_specs=[vmem] * 6,
+        out_shape=tuple(pltpu.VMEM(*shape) for shape in shapes),
+        in_specs=[hbm] * 6,
         out_specs=(vmem,) * 4,
         scratch_shapes=[
-            pltpu.VMEM((rows, 256), BF16),
-            pltpu.VMEM((rows, 128), BF16),
+            pltpu.VMEM((256, rows), BF16),
+            pltpu.VMEM((256, COLS), BF16),
+            pltpu.VMEM((BLOCKS, rows), BF16),
+            pltpu.VMEM((ROWS, COLS), F32),
+            pltpu.VMEM((ROWS, COLS), F32),
+            pltpu.VMEM((ROWS, COLS), F32),
+            pltpu.VMEM((rows, 512), BF16),
+            pltpu.VMEM((rows, 128), F32),
             pltpu.VMEM((TILE, TILE), BF16),
-            pltpu.VMEM((NX, NZ, ROWS, COLS), F32),
-            pltpu.VMEM((CHUNKS, 2, HALF, NX * ROWS, W), BF16),
-            pltpu.VMEM((CHUNKS, 2, HALF, NX * ROWS, W), BF16),
+            pltpu.VMEM((512, COLS), BF16),
+            pltpu.VMEM((NZ, GROUP, COLS), F32),
+            pltpu.VMEM((CHUNKS, 2, HALF, GROUP, W), BF16),
+            pltpu.VMEM((CHUNKS, 2, HALF, GROUP, W), BF16),
             pltpu.VMEM((CHUNKS, NX, ROWS, W), F32),
             pltpu.VMEM((CHUNKS, NX - 1, ROWS, W), F32),
             pltpu.VMEM((CHUNKS, 2 * ROWS, W // 2), BF16),
             pltpu.VMEM((CHUNKS, NMP, 2 * ROWS, W // 2), BF16),
+            dma((5 + CHUNKS,)),
             dma((CHUNKS, 2, HALF)),
             dma((CHUNKS, 2, HALF)),
             dma((CHUNKS, NX - 1)),
@@ -269,7 +310,14 @@
             collective_id=0, has_side_effects=True, vmem_limit_bytes=48 * 2**20
         ),
         cost_estimate=pl.CostEstimate(flops=3 * 10**9, bytes_accessed=4 * 10**6, transcendentals=0),
-    )(activations, cotangent, block_scale.T, master_weight, moment_one, moment_two)
+    )(*args)
+    return pl.pallas_call(
+        write,
+        out_shape=tuple(jax.ShapeDtypeStruct(*shape) for shape in shapes),
+        in_specs=[vmem] * 4,
+        out_specs=(hbm,) * 4,
+        scratch_shapes=[dma((4,))],
+    )(*[pltpu.with_memory_space_constraint(r, pltpu.VMEM) for r in results])
 
 
 def solution(mesh):

time: 73.3 us -> 61.7 us (0.84)
  local copies, waits for them, and re-layouts: 8.43 us -> 0 us
  Pallas kernels: 63.9 us -> 60.9 us
    unnamed x16 -> x0, local copies, waits for them, and re-layouts: 8.43 us -> none
    pallas_call x1 -> x2, Pallas kernels: 63.9 us -> 60.9 us  [the longest x1 60 us: local(): pl.pallas_call(kernel, out_shape=tuple((pltpu.VMEM(*shape) for shape in s...]
where the time goes in v2:
time: 61.7 us; the launch traced here: 61.5 us
  Pallas kernels  60.9 us (99%)
  between operations  0.64 us (1%)
    pallas_call x1, Pallas kernels, local(): pl.pallas_call(kernel, out_shape=tuple((pltpu.VMEM(*shape) for shape in s...  60 us

profile of v2, /device:TPU:1, one launch (start us, length us, event | category | flops | bytes accessed | tf_op | source)
XLA Modules:
  0.0 61.5 jit_solution(10331889493467698647)
XLA Ops:
  0.6 60.0 %shard_map.93 = (bf16[8,24576]{1,0:T(8,128)(2,1)S(1)}, f32[8,3072]{1,0:T(8,128)S(1)}, f32[8,3072]{1,0:T(8,128)S(1)}, f32[8,3072]{1,0:T(8,128)S(1)}) custom-call(bf16[256,512]{1,0:T(8,128)(2,1)} %act_hbm.1, bf16[256,3072]{1,0:T(8,128)(2,1)} %cot_hbm.1, bf16[24,512]{1,0:T(8,128)(2,1)} %bitcast.1, f32[8,3072]{1,0:T(8,128)} %master_hbm.1, f32[8,3072]{1,0:T(8,128)} %one_hbm.1, ...), custom_call_target="tpu_custom_call" | custom-call | flops 3000000000 | bytes 4000000 | tf_op jit(solution)/shard_map/pallas_call | solution.py:278
  60.7 0.9 %shard_map.94 = (bf16[8,24576]{1,0:T(8,128)(2,1)}, f32[8,3072]{1,0:T(8,128)}, f32[8,3072]{1,0:T(8,128)}, f32[8,3072]{1,0:T(8,128)}) custom-call(bf16[8,24576]{1,0:T(8,128)(2,1)S(1)} %get-tuple-element.8.refs_0_, f32[8,3072]{1,0:T(8,128)S(1)} %get-tuple-element.9.refs_1_, f32[8,3072]{1,0:T(8,128)S(1)} %get-tuple-element.10.refs_2_, ...), custom_call_target="tpu_custom_call" | custom-call | tf_op jit(solution)/shard_map/pallas_call | solution.py:314

commit v3 on v2

--- a/solution.py
+++ b/solution.py
@@ -17,6 +17,9 @@
 BLOCKS = COLS // 128
 CHUNKS = 4
 W = COLS // CHUNKS
+SWAP = 2
+WIDE = SWAP * W
+FAR = WIDE // 2
 TILE = 256
 HALF = NZ // 2
 UNIT = 2.0**20
@@ -64,7 +67,9 @@
     weight_out, master_out, one_out, two_out,
     act_ref, cot_ref, scale_ref, master_ref, one_ref, two_ref,
     act_t, scale_t, table, turned, values, ring_out, ring_in, x_out, x_in, w_out, w_in,
+    far_out, far_in, far_values, far_ring_out, far_ring_in,
     load_sem, ring_ss, ring_rs, x_ss, x_rs, w_ss, w_rs,
+    far_ss, far_rs, far_ring_ss, far_ring_rs,
 ):
     dp, mp = lax.axis_index("dp"), lax.axis_index("mp")
     x, z = dp // NZ, lax.rem(dp, NZ)
@@ -85,6 +90,7 @@
         pl.semaphore_signal(barrier, inc=1, device_id=partner)
 
     loads = [(act_hbm, act_ref), (scale_hbm, scale_ref)]
+    near = range(SWAP, CHUNKS)
     for c in range(CHUNKS):
         cols = slice(c * W, (c + 1) * W)
         loads.append((cot_hbm.at[:, cols], cot_ref.at[:, cols]))
@@ -115,20 +121,83 @@
             turned[:256, lo : lo + TILE] = high
             turned[256:, lo : lo + TILE] = low
 
-    def local_rows(targets):
+    def target(d, s):
+        return lax.rem(z + (1 - 2 * d) * (HALF - s) + NZ, NZ)
+
+    def pair(s):
+        return (target(0, 0), z) if isinstance(s, int) and s == 0 else (target(0, s), target(1, s))
+
+    def local_rows(s):
+        targets = pair(s)
         spans = [pl.ds(pl.multiple_of(zd * GROUP, GROUP), GROUP) for zd in targets]
         rows = jnp.concatenate([act_t[span, :] for span in spans], axis=0)
         scales = jnp.concatenate([scale_t[span, :] for span in spans], axis=0)
         inverse = ROOT / scales
         for lo in range(0, COLS, TILE):
             grad = dot(rows, turned[:, lo : lo + TILE])
-            for at in range(0, TILE, 128):
-                b = (lo + at) // 128
-                scaled = grad[:, at : at + 128] * inverse[:, b : b + 1]
+            for at in range(lo, lo + TILE, 128):
+                b = at // 128
+                scaled = grad[:, at - lo : at - lo + 128] * inverse[:, b : b + 1]
                 quant = jnp.clip(scaled, -448.0, 448.0).astype(BF16).astype(F32)
                 value = quant * (scales[:, b : b + 1] * UNIT)
                 for i, zd in enumerate(targets):
-                    values[zd, :, lo + at : lo + at + 128] = value[i * GROUP : (i + 1) * GROUP]
+                    values[zd, :, at : at + 128] = value[i * GROUP : (i + 1) * GROUP]
+                if at < WIDE:
+                    for xd in range(NX):
+                        mine = [value[i * GROUP + xd * ROWS :][:ROWS] for i in range(2)]
+                        far_out[s, xd, :, at : at + 128] = encode(jnp.concatenate(mine, axis=0))
+
+
+    def far_copy(s, j):
+        return pltpu.make_async_remote_copy(
+            src_ref=far_out.at[s, lax.rem(x + j, NX)],
+            dst_ref=far_in.at[s, j - 1],
+            send_sem=far_ss.at[s, j - 1],
+            recv_sem=far_rs.at[s, j - 1],
+            device_id=at_x(j),
+        )
+
+    def far_send(s):
+        for j in (2, 1, 3):
+            far_copy(s, j).start()
+
+    def far_sum(s):
+        span = pl.ds(pl.multiple_of(x * ROWS, ROWS), ROWS)
+        targets = pair(s)
+        for j in range(1, NX):
+            far_copy(s, j).wait_recv()
+        for lo in range(0, WIDE, 128):
+            cols = slice(lo, lo + 128)
+            total = jnp.concatenate([values[zd, span, cols] for zd in targets], axis=0)
+            for j in range(NX - 1):
+                total = total + decode(far_in[s, j, :, cols])
+            for i, zd in enumerate(targets):
+                far_values[zd, :, cols] = total[i * ROWS : (i + 1) * ROWS]
+
+    def far_ring_copy(d, s):
+        return pltpu.make_async_remote_copy(
+            src_ref=far_ring_out.at[d, s],
+            dst_ref=far_ring_in.at[d, s],
+            send_sem=far_ring_ss.at[d, s],
+            recv_sem=far_ring_rs.at[d, s],
+            device_id=at_z(1 - 2 * d),
+        )
+
+    def far_own(zd, lo):
+        halves = [far_values[zd, :, at : at + 128] for at in (lo, FAR + lo)]
+        return jnp.concatenate(halves, axis=0)
+
+    def far_pass_on(d, s, fresh=False):
+        zd = target(d, s)
+        if not fresh:
+            far_ring_copy(d, s - 1).wait_recv()
+        for lo in range(0, FAR, 128):
+            total = far_own(zd, lo)
+            if not fresh:
+                total = total + decode(far_ring_in[d, s - 1, :, lo : lo + 128])
+            far_ring_out[d, s, :, lo : lo + 128] = encode(total)
+        far_ring_copy(d, s).start()
+
 
     def ring_copy(c, d, s, width=W):
         return pltpu.make_async_remote_copy(
@@ -141,9 +210,6 @@
 
     def own(c, zd, lo):
         return values[zd, :, c * W + lo : c * W + lo + 128]
-
-    def target(d, s):
-        return lax.rem(z + (1 - 2 * d) * (HALF - s) + NZ, NZ)
 
     def first(c):
         zd = target(0, 0)
@@ -182,41 +248,8 @@
             device_id=at_mp(j),
         )
 
-    local_rows([target(0, 0)])
-    pl.semaphore_wait(barrier, len(partners))
-    for c in range(CHUNKS):
-        first(c)
-    local_rows([target(0, 1), target(1, 1)])
-    for load in loads[-3:]:
-        load.wait()
-
-    def step(s, near=False):
-        for c in range(CHUNKS):
-            for d in range(2):
-                pass_on(c, d, s, near)
-        local_rows([target(0, s + 1), target(1, s + 1)])
-
-    step(1, True)
-    lax.fori_loop(2, HALF, lambda s, _: (step(s), 0)[1], 0)
-
-    for c in range(CHUNKS):
-        for d in range(2):
-            ring_copy(c, d, HALF - 1).wait_recv()
-        for lo in range(0, W, 128):
-            total = own(c, z, lo) + decode(ring_in[c, 0, HALF - 1, :, lo : lo + 128])
-            total = total + decode(ring_in[c, 1, HALF - 1, :, lo : lo + 128])
-            x_out[c, :, :, lo : lo + 128] = total.reshape(NX, ROWS, 128)
-        for j in (2, 1, 3):
-            x_copy(c, j).start()
-
-    for c in range(CHUNKS):
-        for j in range(1, NX):
-            x_copy(c, j).wait_recv()
-        total = x_out[c, x]
-        for j in range(1, NX):
-            total = total + x_in[c, j - 1]
-        stack = jnp.concatenate([total[:, lo : lo + 128] for lo in range(0, W, 128)], axis=0)
-        pieces = split(stack, 3)
+    def update(c, totals):
+        pieces = split(jnp.concatenate(totals, axis=0), 3)
         back = dot(pieces[0], table[:128, :128])
         back = back + dot(pieces[1], table[:128, :128])
         back = (back + dot(pieces[2], table[:128, :128])) * (ROOT / UNIT)
@@ -240,7 +273,7 @@
             w_copy(c, j, mp).start()
         w_in[c, mp] = w_out[c]
 
-    for c in range(CHUNKS):
+    def gathered(c):
         for j in range(1, NMP):
             w_copy(c, j, lax.rem(mp - j + NMP, NMP)).wait_recv()
         for source in range(NMP):
@@ -249,12 +282,95 @@
             weight_out[:, at : at + W // 2] = both[:ROWS].astype(BF16)
             weight_out[:, at + W // 2 : at + W] = both[ROWS:].astype(BF16)
 
-    for c in range(CHUNKS):
+    def far_step(s):
+        far_sum(s)
+        far_pass_on(0, s)
+        far_pass_on(1, s)
+
+    local_rows(0)
+    pl.semaphore_wait(barrier, len(partners))
+    for c in near:
+        first(c)
+    far_send(0)
+    for s in (1, 2):
+        local_rows(s)
+        far_send(s)
+    for load in loads[-3:]:
+        load.wait()
+
+    def near_step(s, edge=False):
+        for c in near:
+            for d in range(2):
+                pass_on(c, d, s, edge)
+
+    def ahead(s):
+        local_rows(s + 2)
+        far_send(s + 2)
+
+    near_step(1, True)
+    far_sum(0)
+    far_pass_on(0, 0, True)
+    ahead(1)
+    near_step(2)
+    far_sum(1)
+    far_pass_on(0, 1)
+    far_pass_on(1, 1, True)
+    ahead(2)
+
+    def step(s, carry):
+        near_step(s)
+        far_step(s - 1)
+        ahead(s)
+        return carry
+
+    lax.fori_loop(3, HALF - 2, step, 0)
+    for s in (HALF - 2, HALF - 1):
+        near_step(s)
+        far_step(s - 1)
+
+    for c in near:
+        for d in range(2):
+            ring_copy(c, d, HALF - 1).wait_recv()
+        for lo in range(0, W, 128):
+            total = own(c, z, lo) + decode(ring_in[c, 0, HALF - 1, :, lo : lo + 128])
+            total = total + decode(ring_in[c, 1, HALF - 1, :, lo : lo + 128])
+            x_out[c, :, :, lo : lo + 128] = total.reshape(NX, ROWS, 128)
+        for j in (2, 1, 3):
+            x_copy(c, j).start()
+    far_step(HALF - 1)
+
+    for c in near:
+        for j in range(1, NX):
+            x_copy(c, j).wait_recv()
+        total = x_out[c, x]
+        for j in range(1, NX):
+            total = total + x_in[c, j - 1]
+        update(c, [total[:, lo : lo + 128] for lo in range(0, W, 128)])
+
+    for d in range(2):
+        far_ring_copy(d, HALF - 1).wait_recv()
+    totals = []
+    for lo in range(0, FAR, 128):
+        total = far_own(z, lo) + decode(far_ring_in[0, HALF - 1, :, lo : lo + 128])
+        totals.append(total + decode(far_ring_in[1, HALF - 1, :, lo : lo + 128]))
+    totals = [t[:ROWS] for t in totals] + [t[ROWS:] for t in totals]
+    for c in range(SWAP):
+        update(c, totals[c * W // 128 : (c + 1) * W // 128])
+
+    for c in (*near, *range(SWAP)):
+        gathered(c)
+
+    for j in range(1, NX):
+        lax.fori_loop(0, HALF, lambda s, _: (far_copy(s, j).wait_send(), 0)[1], 0)
+    for d in range(2):
+        lax.fori_loop(d, HALF, lambda s, _: (far_ring_copy(d, s).wait_send(), 0)[1], 0)
+    for c in near:
         for d in range(2):
             ring_copy(c, d, 0, W // 2).wait_send()
             lax.fori_loop(1, HALF, lambda s, _: (ring_copy(c, d, s).wait_send(), 0)[1], 0)
         for j in range(1, NX):
             x_copy(c, j).wait_send()
+    for c in range(CHUNKS):
         for j in range(1, NMP):
             w_copy(c, j, mp).wait_send()
 
@@ -298,6 +414,11 @@
             pltpu.VMEM((CHUNKS, NX - 1, ROWS, W), F32),
             pltpu.VMEM((CHUNKS, 2 * ROWS, W // 2), BF16),
             pltpu.VMEM((CHUNKS, NMP, 2 * ROWS, W // 2), BF16),
+            pltpu.VMEM((HALF, NX, 2 * ROWS, WIDE), BF16),
+            pltpu.VMEM((HALF, NX - 1, 2 * ROWS, WIDE), BF16),
+            pltpu.VMEM((NZ, ROWS, WIDE), F32),
+            pltpu.VMEM((2, HALF, 2 * ROWS, FAR), BF16),
+            pltpu.VMEM((2, HALF, 2 * ROWS, FAR), BF16),
             dma((5 + CHUNKS,)),
             dma((CHUNKS, 2, HALF)),
             dma((CHUNKS, 2, HALF)),
@@ -305,6 +426,10 @@
             dma((CHUNKS, NX - 1)),
             dma((CHUNKS, NMP - 1)),
             dma((CHUNKS, NMP)),
+            dma((HALF, NX - 1)),
+            dma((HALF, NX - 1)),
+            dma((2, HALF)),
+            dma((2, HALF)),
         ],
         compiler_params=pltpu.CompilerParams(
             collective_id=0, has_side_effects=True, vmem_limit_bytes=48 * 2**20

time: 61.7 us -> 58.3 us (0.945)
  Pallas kernels: 60.9 us -> 57.6 us
    pallas_call x1, Pallas kernels: 60 us -> 56.7 us  [local(): pl.pallas_call(kernel, out_shape=tuple((pltpu.VMEM(*shape) for shape in s...]
where the time goes in v3:
time: 58.3 us; the launch traced here: 58.2 us
  Pallas kernels  57.6 us (99%)
  between operations  0.64 us (1%)
    pallas_call x1, Pallas kernels, local(): pl.pallas_call(kernel, out_shape=tuple((pltpu.VMEM(*shape) for shape in s...  56.7 us

profile of v3, /device:TPU:1, one launch (start us, length us, event | category | flops | bytes accessed | tf_op | source)
XLA Modules:
  0.0 58.2 jit_solution(7827207445055934690)
XLA Ops:
  0.6 56.7 %shard_map.93 = (bf16[8,24576]{1,0:T(8,128)(2,1)S(1)}, f32[8,3072]{1,0:T(8,128)S(1)}, f32[8,3072]{1,0:T(8,128)S(1)}, f32[8,3072]{1,0:T(8,128)S(1)}) custom-call(bf16[256,512]{1,0:T(8,128)(2,1)} %act_hbm.1, bf16[256,3072]{1,0:T(8,128)(2,1)} %cot_hbm.1, bf16[24,512]{1,0:T(8,128)(2,1)} %bitcast.1, f32[8,3072]{1,0:T(8,128)} %master_hbm.1, f32[8,3072]{1,0:T(8,128)} %one_hbm.1, ...), custom_call_target="tpu_custom_call" | custom-call | flops 3000000000 | bytes 4000000 | tf_op jit(solution)/shard_map/pallas_call | solution.py:394
  57.3 0.9 %shard_map.94 = (bf16[8,24576]{1,0:T(8,128)(2,1)}, f32[8,3072]{1,0:T(8,128)}, f32[8,3072]{1,0:T(8,128)}, f32[8,3072]{1,0:T(8,128)}) custom-call(bf16[8,24576]{1,0:T(8,128)(2,1)S(1)} %get-tuple-element.8.refs_0_, f32[8,3072]{1,0:T(8,128)S(1)} %get-tuple-element.9.refs_1_, f32[8,3072]{1,0:T(8,128)S(1)} %get-tuple-element.10.refs_2_, ...), custom_call_target="tpu_custom_call" | custom-call | tf_op jit(solution)/shard_map/pallas_call | solution.py:439

commit v4 on v3

--- a/solution.py
+++ b/solution.py
@@ -15,13 +15,13 @@
 GROUP = NX * ROWS
 COLS = 3072
 BLOCKS = COLS // 128
-CHUNKS = 4
-W = COLS // CHUNKS
-SWAP = 2
-WIDE = SWAP * W
+WIDE = 2048
 FAR = WIDE // 2
+NEAR = 2
+W = (COLS - WIDE) // NEAR
 TILE = 256
 HALF = NZ // 2
+NEAR_FRESH, FAR_FRESH = (1, 7), (1, 3, 5, 7)
 UNIT = 2.0**20
 ROOT = 1.0 / math.sqrt(128.0)
 F32, BF16 = jnp.float32, jnp.bfloat16
@@ -36,6 +36,16 @@
     size = jnp.maximum(jnp.abs(y), 2.0**-124)
     r = lax.rsqrt(size)
     return y * (r * lax.rsqrt(size * r))
+
+
+def reach(fresh, s):
+    return 1 if s in fresh or s + 1 not in fresh else 2
+
+
+def sources(fresh, s):
+    if s in fresh or s == 0:
+        return []
+    return [s - 1, s - 2] if s - 1 in fresh else [s - 1]
 
 
 def split(x, parts):
@@ -83,21 +93,21 @@
     def at_mp(step):
         return {"mp": lax.rem(mp + step + NMP, NMP)}
 
-    barrier = pltpu.get_barrier_semaphore()
-    partners = [at_z(1), at_z(-1)]
-    partners += [at_x(j) for j in range(1, NX)] + [at_mp(j) for j in range(1, NMP)]
-    for partner in partners:
-        pl.semaphore_signal(barrier, inc=1, device_id=partner)
-
     loads = [(act_hbm, act_ref), (scale_hbm, scale_ref)]
-    near = range(SWAP, CHUNKS)
-    for c in range(CHUNKS):
-        cols = slice(c * W, (c + 1) * W)
-        loads.append((cot_hbm.at[:, cols], cot_ref.at[:, cols]))
+    near = range(NEAR)
+    pieces = ((0, 768), (768, WIDE), (WIDE, COLS))
+    for lo, hi in pieces:
+        loads.append((cot_hbm.at[:, lo:hi], cot_ref.at[:, lo:hi]))
     loads += [(one_hbm, one_ref), (two_hbm, two_ref), (master_hbm, master_ref)]
     loads = [pltpu.make_async_copy(s, d, load_sem.at[i]) for i, (s, d) in enumerate(loads)]
     for load in loads:
         load.start()
+
+    barrier = pltpu.get_barrier_semaphore()
+    partners = [at_z(j) for j in (1, -1, 2, -2)]
+    partners += [at_x(j) for j in range(1, NX)] + [at_mp(j) for j in range(1, NMP)]
+    for partner in partners:
+        pl.semaphore_signal(barrier, inc=1, device_id=partner)
 
     table[...] = signs(TILE)
     loads[0].wait()
@@ -114,9 +124,9 @@
         for xd in range(NX):
             at = (xd * NZ + zd) * ROWS
             scale_t[zd * GROUP + xd * ROWS : zd * GROUP + (xd + 1) * ROWS, :] = scale[at : at + ROWS]
-    for c in range(CHUNKS):
-        loads[2 + c].wait()
-        for lo in range(c * W, (c + 1) * W, TILE):
+    def turn(piece):
+        loads[2 + piece].wait()
+        for lo in range(*pieces[piece], TILE):
             high, low = split(dot(cot_ref[:, lo : lo + TILE], table[...]), 2)
             turned[:256, lo : lo + TILE] = high
             turned[256:, lo : lo + TILE] = low
@@ -127,13 +137,13 @@
     def pair(s):
         return (target(0, 0), z) if isinstance(s, int) and s == 0 else (target(0, s), target(1, s))
 
-    def local_rows(s):
+    def local_rows(s, begin=0, end=COLS):
         targets = pair(s)
         spans = [pl.ds(pl.multiple_of(zd * GROUP, GROUP), GROUP) for zd in targets]
         rows = jnp.concatenate([act_t[span, :] for span in spans], axis=0)
         scales = jnp.concatenate([scale_t[span, :] for span in spans], axis=0)
         inverse = ROOT / scales
-        for lo in range(0, COLS, TILE):
+        for lo in range(begin, end, TILE):
             grad = dot(rows, turned[:, lo : lo + TILE])
             for at in range(lo, lo + TILE, 128):
                 b = at // 128
@@ -180,21 +190,22 @@
             dst_ref=far_ring_in.at[d, s],
             send_sem=far_ring_ss.at[d, s],
             recv_sem=far_ring_rs.at[d, s],
-            device_id=at_z(1 - 2 * d),
+            device_id=at_z((1 - 2 * d) * reach(FAR_FRESH, s)),
         )
 
     def far_own(zd, lo):
         halves = [far_values[zd, :, at : at + 128] for at in (lo, FAR + lo)]
         return jnp.concatenate(halves, axis=0)
 
-    def far_pass_on(d, s, fresh=False):
+    def far_pass_on(d, s):
         zd = target(d, s)
-        if not fresh:
-            far_ring_copy(d, s - 1).wait_recv()
+        arrived = [t for t in sources(FAR_FRESH, s) if t or not d]
+        for t in arrived:
+            far_ring_copy(d, t).wait_recv()
         for lo in range(0, FAR, 128):
             total = far_own(zd, lo)
-            if not fresh:
-                total = total + decode(far_ring_in[d, s - 1, :, lo : lo + 128])
+            for t in arrived:
+                total = total + decode(far_ring_in[d, t, :, lo : lo + 128])
             far_ring_out[d, s, :, lo : lo + 128] = encode(total)
         far_ring_copy(d, s).start()
 
@@ -205,28 +216,45 @@
             dst_ref=ring_in.at[c, d, s, :, pl.ds(0, width)],
             send_sem=ring_ss.at[c, d, s],
             recv_sem=ring_rs.at[c, d, s],
-            device_id=at_z(1 - 2 * d),
+            device_id=at_z((1 - 2 * d) * reach(NEAR_FRESH, s)),
         )
 
     def own(c, zd, lo):
-        return values[zd, :, c * W + lo : c * W + lo + 128]
+        return values[zd, :, WIDE + c * W + lo : WIDE + c * W + lo + 128]
+
+    def share(c, d):
+        middle = (W // 256 + c % 2) * 128
+        return (0, middle) if d == 0 else (middle, W)
+
+    def width(c, d, s):
+        begin, end = (0, W) if s else share(c, d)
+        return end - begin
 
     def first(c):
         zd = target(0, 0)
         for d in range(2):
-            for lo in range(0, W // 2, 128):
-                ring_out[c, d, 0, :, lo : lo + 128] = encode(own(c, zd, lo + d * (W // 2)))
-            ring_copy(c, d, 0, W // 2).start()
-
-    def pass_on(c, d, s, near=False):
+            begin, end = share(c, d)
+            for lo in range(begin, end, 128):
+                ring_out[c, d, 0, :, lo - begin : lo - begin + 128] = encode(own(c, zd, lo))
+            ring_copy(c, d, 0, end - begin).start()
+
+    def arrivals(c, d, s, lo):
+        for t in sources(NEAR_FRESH, s):
+            begin, end = (0, W) if t else share(c, d)
+            if begin <= lo < end:
+                yield decode(ring_in[c, d, t, :, lo - begin : lo - begin + 128])
+
+    def await_arrivals(c, d, s):
+        for t in sources(NEAR_FRESH, s):
+            ring_copy(c, d, t, width(c, d, t)).wait_recv()
+
+    def pass_on(c, d, s):
         zd = target(d, s)
-        begin, width = (d * (W // 2), W // 2) if near else (0, W)
-        ring_copy(c, d, s - 1, width).wait_recv()
+        await_arrivals(c, d, s)
         for lo in range(0, W, 128):
             total = own(c, zd, lo)
-            if begin <= lo < begin + width:
-                at = lo - begin
-                total = total + decode(ring_in[c, d, s - 1, :, at : at + 128])
+            for term in arrivals(c, d, s, lo):
+                total = total + term
             ring_out[c, d, s, :, lo : lo + 128] = encode(total)
         ring_copy(c, d, s).start()
 
@@ -239,23 +267,26 @@
             device_id=at_x(j),
         )
 
-    def w_copy(c, j, slot):
+    def w_copy(lanes, j, slot):
         return pltpu.make_async_remote_copy(
-            src_ref=w_out.at[c],
-            dst_ref=w_in.at[c, slot],
-            send_sem=w_ss.at[c, j - 1],
-            recv_sem=w_rs.at[c, slot],
+            src_ref=w_out.at[:, lanes],
+            dst_ref=w_in.at[slot, :, lanes],
+            send_sem=w_ss.at[min(lanes.start, 1), j - 1],
+            recv_sem=w_rs.at[min(lanes.start, 1), slot],
             device_id=at_mp(j),
         )
 
-    def update(c, totals):
+    near_lanes, far_lanes = pl.ds(FAR, COLS // 2 - FAR), pl.ds(0, FAR)
+
+    def update(begin, totals, lanes):
+        count = len(totals)
         pieces = split(jnp.concatenate(totals, axis=0), 3)
         back = dot(pieces[0], table[:128, :128])
         back = back + dot(pieces[1], table[:128, :128])
         back = (back + dot(pieces[2], table[:128, :128])) * (ROOT / UNIT)
         blocks = []
-        for b in range(W // 128):
-            cols = slice(c * W + b * 128, c * W + (b + 1) * 128)
+        for b in range(count):
+            cols = slice(begin + b * 128, begin + (b + 1) * 128)
             gradient = back[b * ROWS : (b + 1) * ROWS, :]
             one = 0.9 * one_ref[:, cols] + 0.1 * gradient
             two = 0.95 * two_ref[:, cols] + 0.05 * gradient * gradient
@@ -266,113 +297,125 @@
             two_out[:, cols] = two
             master_out[:, cols] = master
             blocks.append(master)
-        for b in range(W // 256):
-            pair = jnp.concatenate([blocks[b], blocks[b + W // 256]], axis=0).astype(BF16)
-            w_out[c, :, b * 128 : (b + 1) * 128] = pair
+        for b in range(count // 2):
+            both = jnp.concatenate([blocks[b], blocks[b + count // 2]], axis=0).astype(BF16)
+            at = begin // 2 + b * 128
+            w_out[:, at : at + 128] = both
+            w_in[mp, :, at : at + 128] = both
         for j in range(1, NMP):
-            w_copy(c, j, mp).start()
-        w_in[c, mp] = w_out[c]
-
-    def gathered(c):
+            w_copy(lanes, j, mp).start()
+
+    def gathered(begin, end, lanes):
         for j in range(1, NMP):
-            w_copy(c, j, lax.rem(mp - j + NMP, NMP)).wait_recv()
+            w_copy(lanes, j, lax.rem(mp - j + NMP, NMP)).wait_recv()
+        half = (end - begin) // 2
         for source in range(NMP):
-            both = w_in[c, source].astype(F32)
-            at = source * COLS + c * W
-            weight_out[:, at : at + W // 2] = both[:ROWS].astype(BF16)
-            weight_out[:, at + W // 2 : at + W] = both[ROWS:].astype(BF16)
+            both = w_in[source, :, begin // 2 : end // 2].astype(F32)
+            at = source * COLS + begin
+            weight_out[:, at : at + half] = both[:ROWS].astype(BF16)
+            weight_out[:, at + half : at + 2 * half] = both[ROWS:].astype(BF16)
 
     def far_step(s):
         far_sum(s)
-        far_pass_on(0, s)
-        far_pass_on(1, s)
-
-    local_rows(0)
+        for d in range(2):
+            if s or not d:
+                far_pass_on(d, s)
+
+    def near_step(s):
+        for c in near:
+            for d in range(2):
+                pass_on(c, d, s)
+
+    def rows_of(s):
+        local_rows(s)
+        far_send(s)
+
+    turn(0)
+    turn(1)
+    local_rows(0, 0, WIDE)
     pl.semaphore_wait(barrier, len(partners))
+    far_send(0)
+    turn(2)
+    local_rows(0, WIDE, COLS)
     for c in near:
         first(c)
-    far_send(0)
-    for s in (1, 2):
-        local_rows(s)
-        far_send(s)
+    for s in (1, 2, 3):
+        rows_of(s)
+        if s == 1:
+            near_step(1)
     for load in loads[-3:]:
         load.wait()
 
-    def near_step(s, edge=False):
-        for c in near:
-            for d in range(2):
-                pass_on(c, d, s, edge)
-
-    def ahead(s):
-        local_rows(s + 2)
-        far_send(s + 2)
-
-    near_step(1, True)
-    far_sum(0)
-    far_pass_on(0, 0, True)
-    ahead(1)
     near_step(2)
-    far_sum(1)
-    far_pass_on(0, 1)
-    far_pass_on(1, 1, True)
-    ahead(2)
-
-    def step(s, carry):
-        near_step(s)
-        far_step(s - 1)
-        ahead(s)
-        return carry
-
-    lax.fori_loop(3, HALF - 2, step, 0)
-    for s in (HALF - 2, HALF - 1):
-        near_step(s)
-        far_step(s - 1)
+    far_step(0)
+    rows_of(4)
+    near_step(3)
+    far_step(1)
+    rows_of(5)
+    near_step(4)
+    far_step(2)
+    rows_of(6)
+    near_step(5)
+    far_step(3)
+    rows_of(7)
+    near_step(7)
+    near_step(6)
+    far_step(4)
+    far_step(5)
 
     for c in near:
         for d in range(2):
-            ring_copy(c, d, HALF - 1).wait_recv()
+            await_arrivals(c, d, HALF)
         for lo in range(0, W, 128):
-            total = own(c, z, lo) + decode(ring_in[c, 0, HALF - 1, :, lo : lo + 128])
-            total = total + decode(ring_in[c, 1, HALF - 1, :, lo : lo + 128])
+            total = own(c, z, lo)
+            for d in range(2):
+                for term in arrivals(c, d, HALF, lo):
+                    total = total + term
             x_out[c, :, :, lo : lo + 128] = total.reshape(NX, ROWS, 128)
         for j in (2, 1, 3):
             x_copy(c, j).start()
-    far_step(HALF - 1)
-
+    far_step(6)
+    far_step(7)
+
+    totals = []
     for c in near:
         for j in range(1, NX):
             x_copy(c, j).wait_recv()
         total = x_out[c, x]
         for j in range(1, NX):
             total = total + x_in[c, j - 1]
-        update(c, [total[:, lo : lo + 128] for lo in range(0, W, 128)])
-
+        totals += [total[:, lo : lo + 128] for lo in range(0, W, 128)]
+    update(WIDE, totals, near_lanes)
+
+    totals = []
     for d in range(2):
-        far_ring_copy(d, HALF - 1).wait_recv()
-    totals = []
+        for t in sources(FAR_FRESH, HALF):
+            far_ring_copy(d, t).wait_recv()
     for lo in range(0, FAR, 128):
-        total = far_own(z, lo) + decode(far_ring_in[0, HALF - 1, :, lo : lo + 128])
-        totals.append(total + decode(far_ring_in[1, HALF - 1, :, lo : lo + 128]))
-    totals = [t[:ROWS] for t in totals] + [t[ROWS:] for t in totals]
-    for c in range(SWAP):
-        update(c, totals[c * W // 128 : (c + 1) * W // 128])
-
-    for c in (*near, *range(SWAP)):
-        gathered(c)
+        total = far_own(z, lo)
+        for d in range(2):
+            for t in sources(FAR_FRESH, HALF):
+                total = total + decode(far_ring_in[d, t, :, lo : lo + 128])
+        totals.append(total)
+    update(0, [t[:ROWS] for t in totals] + [t[ROWS:] for t in totals], far_lanes)
+
+    gathered(WIDE, COLS, near_lanes)
+    gathered(0, WIDE, far_lanes)
 
     for j in range(1, NX):
         lax.fori_loop(0, HALF, lambda s, _: (far_copy(s, j).wait_send(), 0)[1], 0)
     for d in range(2):
-        lax.fori_loop(d, HALF, lambda s, _: (far_ring_copy(d, s).wait_send(), 0)[1], 0)
+        for s in range(d, HALF):
+            far_ring_copy(d, s).wait_send()
     for c in near:
         for d in range(2):
-            ring_copy(c, d, 0, W // 2).wait_send()
-            lax.fori_loop(1, HALF, lambda s, _: (ring_copy(c, d, s).wait_send(), 0)[1], 0)
+            for s in range(HALF):
+                ring_copy(c, d, s, width(c, d, s)).wait_send()
         for j in range(1, NX):
             x_copy(c, j).wait_send()
-    for c in range(CHUNKS):
-        for j in range(1, NMP):
-            w_copy(c, j, mp).wait_send()
+    for j in range(1, NMP):
+        w_copy(near_lanes, j, mp).wait_send()
+        w_copy(far_lanes, j, mp).wait_send()
 
 
 def write(*refs):
@@ -408,24 +451,24 @@
             pltpu.VMEM((TILE, TILE), BF16),
             pltpu.VMEM((512, COLS), BF16),
             pltpu.VMEM((NZ, GROUP, COLS), F32),
-            pltpu.VMEM((CHUNKS, 2, HALF, GROUP, W), BF16),
-            pltpu.VMEM((CHUNKS, 2, HALF, GROUP, W), BF16),
-            pltpu.VMEM((CHUNKS, NX, ROWS, W), F32),
-            pltpu.VMEM((CHUNKS, NX - 1, ROWS, W), F32),
-            pltpu.VMEM((CHUNKS, 2 * ROWS, W // 2), BF16),
-            pltpu.VMEM((CHUNKS, NMP, 2 * ROWS, W // 2), BF16),
+            pltpu.VMEM((NEAR, 2, HALF, GROUP, W), BF16),
+            pltpu.VMEM((NEAR, 2, HALF, GROUP, W), BF16),
+            pltpu.VMEM((NEAR, NX, ROWS, W), F32),
+            pltpu.VMEM((NEAR, NX - 1, ROWS, W), F32),
+            pltpu.VMEM((2 * ROWS, COLS // 2), BF16),
+            pltpu.VMEM((NMP, 2 * ROWS, COLS // 2), BF16),
             pltpu.VMEM((HALF, NX, 2 * ROWS, WIDE), BF16),
             pltpu.VMEM((HALF, NX - 1, 2 * ROWS, WIDE), BF16),
             pltpu.VMEM((NZ, ROWS, WIDE), F32),
             pltpu.VMEM((2, HALF, 2 * ROWS, FAR), BF16),
             pltpu.VMEM((2, HALF, 2 * ROWS, FAR), BF16),
-            dma((5 + CHUNKS,)),
-            dma((CHUNKS, 2, HALF)),
-            dma((CHUNKS, 2, HALF)),
-            dma((CHUNKS, NX - 1)),
-            dma((CHUNKS, NX - 1)),
-            dma((CHUNKS, NMP - 1)),
-            dma((CHUNKS, NMP)),
+            dma((8,)),
+            dma((NEAR, 2, HALF)),
+            dma((NEAR, 2, HALF)),
+            dma((NEAR, NX - 1)),
+            dma((NEAR, NX - 1)),
+            dma((2, NMP - 1)),
+            dma((2, NMP)),
             dma((HALF, NX - 1)),
             dma((HALF, NX - 1)),
             dma((2, HALF)),

time: 58.3 us -> 52.8 us (0.906)
  Pallas kernels: 57.6 us -> 52 us
    pallas_call x1, Pallas kernels: 56.7 us -> 51.1 us  [local(): pl.pallas_call(kernel, out_shape=tuple((pltpu.VMEM(*shape) for shape in s...]
where the time goes in v4:
time: 52.8 us; the launch traced here: 52.7 us
  Pallas kernels  52 us (98%)
  between operations  0.64 us (1%)
    pallas_call x1, Pallas kernels, local(): pl.pallas_call(kernel, out_shape=tuple((pltpu.VMEM(*shape) for shape in s...  51.1 us

profile of v4, /device:TPU:1, one launch (start us, length us, event | category | flops | bytes accessed | tf_op | source)
XLA Modules:
  0.0 52.7 jit_solution(6706848629971281660)
XLA Ops:
  0.6 51.1 %shard_map.93 = (bf16[8,24576]{1,0:T(8,128)(2,1)S(1)}, f32[8,3072]{1,0:T(8,128)S(1)}, f32[8,3072]{1,0:T(8,128)S(1)}, f32[8,3072]{1,0:T(8,128)S(1)}) custom-call(bf16[256,512]{1,0:T(8,128)(2,1)} %act_hbm.1, bf16[256,3072]{1,0:T(8,128)(2,1)} %cot_hbm.1, bf16[24,512]{1,0:T(8,128)(2,1)} %bitcast.1, f32[8,3072]{1,0:T(8,128)} %master_hbm.1, f32[8,3072]{1,0:T(8,128)} %one_hbm.1, ...), custom_call_target="tpu_custom_call" | custom-call | flops 3000000000 | bytes 4000000 | tf_op jit(solution)/shard_map/pallas_call | solution.py:437
  51.8 0.9 %shard_map.94 = (bf16[8,24576]{1,0:T(8,128)(2,1)}, f32[8,3072]{1,0:T(8,128)}, f32[8,3072]{1,0:T(8,128)}, f32[8,3072]{1,0:T(8,128)}) custom-call(bf16[8,24576]{1,0:T(8,128)(2,1)S(1)} %get-tuple-element.8.refs_0_, f32[8,3072]{1,0:T(8,128)S(1)} %get-tuple-element.9.refs_1_, f32[8,3072]{1,0:T(8,128)S(1)} %get-tuple-element.10.refs_2_, ...), custom_call_target="tpu_custom_call" | custom-call | tf_op jit(solution)/shard_map/pallas_call | solution.py:482

commit v5 on v4

--- a/solution.py
+++ b/solution.py
@@ -302,18 +302,19 @@
             at = begin // 2 + b * 128
             w_out[:, at : at + 128] = both
             w_in[mp, :, at : at + 128] = both
-        for j in range(1, NMP):
+        for j in (4, 3, 5, 2, 6, 1, 7):
             w_copy(lanes, j, mp).start()
 
     def gathered(begin, end, lanes):
-        for j in range(1, NMP):
-            w_copy(lanes, j, lax.rem(mp - j + NMP, NMP)).wait_recv()
         half = (end - begin) // 2
-        for source in range(NMP):
+        for j in (0, 1, 7, 2, 6, 3, 5, 4):
+            source = lax.rem(mp - j + NMP, NMP)
+            if j:
+                w_copy(lanes, j, source).wait_recv()
             both = w_in[source, :, begin // 2 : end // 2].astype(F32)
-            at = source * COLS + begin
-            weight_out[:, at : at + half] = both[:ROWS].astype(BF16)
-            weight_out[:, at + half : at + 2 * half] = both[ROWS:].astype(BF16)
+            at = pl.multiple_of(source * COLS + begin, 128)
+            weight_out[:, pl.ds(at, half)] = both[:ROWS].astype(BF16)
+            weight_out[:, pl.ds(at + half, half)] = both[ROWS:].astype(BF16)
 
     def far_step(s):
         far_sum(s)
@@ -339,7 +340,7 @@
     local_rows(0, WIDE, COLS)
     for c in near:
         first(c)
-    for s in (1, 2, 3):
+    for s in (1, 2):
         rows_of(s)
         if s == 1:
             near_step(1)
@@ -347,6 +348,7 @@
         load.wait()
 
     near_step(2)
+    rows_of(3)
     far_step(0)
     rows_of(4)
     near_step(3)
@@ -399,9 +401,6 @@
         totals.append(total)
     update(0, [t[:ROWS] for t in totals] + [t[ROWS:] for t in totals], far_lanes)
 
-    gathered(WIDE, COLS, near_lanes)
-    gathered(0, WIDE, far_lanes)
-
     for j in range(1, NX):
         lax.fori_loop(0, HALF, lambda s, _: (far_copy(s, j).wait_send(), 0)[1], 0)
     for d in range(2):
@@ -413,6 +412,9 @@
                 ring_copy(c, d, s, width(c, d, s)).wait_send()
         for j in range(1, NX):
             x_copy(c, j).wait_send()
+    gathered(WIDE, COLS, near_lanes)
+    gathered(0, WIDE, far_lanes)
+
     for j in range(1, NMP):
         w_copy(near_lanes, j, mp).wait_send()
         w_copy(far_lanes, j, mp).wait_send()

time: 52.8 us -> 52.1 us (0.987)
  Pallas kernels: 52 us -> 51.3 us
    pallas_call x1, Pallas kernels: 51.1 us -> 50.4 us  [local(): pl.pallas_call(kernel, out_shape=tuple((pltpu.VMEM(*shape) for shape in s...]
where the time goes in v5:
time: 52.1 us; the launch traced here: 51.9 us
  Pallas kernels  51.3 us (98%)
  between operations  0.64 us (1%)
    pallas_call x1, Pallas kernels, local(): pl.pallas_call(kernel, out_shape=tuple((pltpu.VMEM(*shape) for shape in s...  50.4 us

profile of v5, /device:TPU:1, one launch (start us, length us, event | category | flops | bytes accessed | tf_op | source)
XLA Modules:
  0.0 51.9 jit_solution(9371438225919051771)
XLA Ops:
  0.6 50.4 %shard_map.93 = (bf16[8,24576]{1,0:T(8,128)(2,1)S(1)}, f32[8,3072]{1,0:T(8,128)S(1)}, f32[8,3072]{1,0:T(8,128)S(1)}, f32[8,3072]{1,0:T(8,128)S(1)}) custom-call(bf16[256,512]{1,0:T(8,128)(2,1)} %act_hbm.1, bf16[256,3072]{1,0:T(8,128)(2,1)} %cot_hbm.1, bf16[24,512]{1,0:T(8,128)(2,1)} %bitcast.1, f32[8,3072]{1,0:T(8,128)} %master_hbm.1, f32[8,3072]{1,0:T(8,128)} %one_hbm.1, ...), custom_call_target="tpu_custom_call" | custom-call | flops 3000000000 | bytes 4000000 | tf_op jit(solution)/shard_map/pallas_call | solution.py:439
  51.1 0.9 %shard_map.94 = (bf16[8,24576]{1,0:T(8,128)(2,1)}, f32[8,3072]{1,0:T(8,128)}, f32[8,3072]{1,0:T(8,128)}, f32[8,3072]{1,0:T(8,128)}) custom-call(bf16[8,24576]{1,0:T(8,128)(2,1)S(1)} %get-tuple-element.8.refs_0_, f32[8,3072]{1,0:T(8,128)S(1)} %get-tuple-element.9.refs_1_, f32[8,3072]{1,0:T(8,128)S(1)} %get-tuple-element.10.refs_2_, ...), custom_call_target="tpu_custom_call" | custom-call | tf_op jit(solution)/shard_map/pallas_call | solution.py:484

commit v6 on v5

--- a/solution.py
+++ b/solution.py
@@ -168,7 +168,7 @@
         )
 
     def far_send(s):
-        for j in (2, 1, 3):
+        for j in (1, 3, 2):
             far_copy(s, j).start()
 
     def far_sum(s):

time: 52.1 us -> 52.7 us (1.012)
  Pallas kernels: 51.3 us -> 51.9 us
    pallas_call x1, Pallas kernels: 50.4 us -> 51 us  [local(): pl.pallas_call(kernel, out_shape=tuple((pltpu.VMEM(*shape) for shape in s...]
where the time goes in v6:
time: 52.7 us; the launch traced here: 52.5 us
  Pallas kernels  51.9 us (98%)
  between operations  0.64 us (1%)
    pallas_call x1, Pallas kernels, local(): pl.pallas_call(kernel, out_shape=tuple((pltpu.VMEM(*shape) for shape in s...  51 us

profile of v6, /device:TPU:1, one launch (start us, length us, event | category | flops | bytes accessed | tf_op | source)
XLA Modules:
  0.0 52.5 jit_solution(10637173123743381141)
XLA Ops:
  0.6 51.0 %shard_map.93 = (bf16[8,24576]{1,0:T(8,128)(2,1)S(1)}, f32[8,3072]{1,0:T(8,128)S(1)}, f32[8,3072]{1,0:T(8,128)S(1)}, f32[8,3072]{1,0:T(8,128)S(1)}) custom-call(bf16[256,512]{1,0:T(8,128)(2,1)} %act_hbm.1, bf16[256,3072]{1,0:T(8,128)(2,1)} %cot_hbm.1, bf16[24,512]{1,0:T(8,128)(2,1)} %bitcast.1, f32[8,3072]{1,0:T(8,128)} %master_hbm.1, f32[8,3072]{1,0:T(8,128)} %one_hbm.1, ...), custom_call_target="tpu_custom_call" | custom-call | flops 3000000000 | bytes 4000000 | tf_op jit(solution)/shard_map/pallas_call | solution.py:439
  51.7 0.9 %shard_map.94 = (bf16[8,24576]{1,0:T(8,128)(2,1)}, f32[8,3072]{1,0:T(8,128)}, f32[8,3072]{1,0:T(8,128)}, f32[8,3072]{1,0:T(8,128)}) custom-call(bf16[8,24576]{1,0:T(8,128)(2,1)S(1)} %get-tuple-element.8.refs_0_, f32[8,3072]{1,0:T(8,128)S(1)} %get-tuple-element.9.refs_1_, f32[8,3072]{1,0:T(8,128)S(1)} %get-tuple-element.10.refs_2_, ...), custom_call_target="tpu_custom_call" | custom-call | tf_op jit(solution)/shard_map/pallas_call | solution.py:484
